TPU v7x, 32 devices: a whole 2x2x4 slice. The times are simulated.
32 devices in a mesh: stn: 16 (over z, y, core), seg: 2 (over x).
Axes of the slice: x: 2, y: 2, z: 4, core: 2. Of those that a mesh axis runs over, the one named last changes fastest.
Arguments:
- spectra: bfloat16 [2, 32, 2, 4096], P('seg', 'stn'), may hold values from -60 to 60, as said below
- flags: int32 [32], P('stn'), may hold values 0 or 1
- pair_first: int32 [16, 16, 4], P('stn'), may hold values from 0 to 1
- pair_second: int32 [16, 16, 4], P('stn'), may hold values from 0 to 1
- owners: int32 [16, 16, 4, 1], P('stn'), may hold values from 0 to 15; in each aligned block of 64 rows (0 to 63, 64 to 127, ..., all dimensions but the last counted through in order) at most 8 rows name the same one
Outputs:
- stacks: float32 [16, 16, 8, 1024], P('stn', None, None, 'seg')
Inputs may be any that keep to these rules, and one draw needn't show every extreme that they name: `spectra`: spectra of one station vary in scale from band to band. `owners`: at most 8 pairs of one source block name the same owner; in every draw some source block gives exactly 8 pairs to one owner.
All inputs are finite; a program needn't handle non-finite values. No bound on the sum of `flags` on one device may be relied on, other than what follows from the above.
Results may differ from a plain program's by a relative error of at most 0.018.
Values may be sent and summed in bfloat16 or wider, within the bound.
A program may use at most 128 MiB of HBM per device.

v0:
```python
import math

import jax
import jax.numpy as jnp
from jax import lax
from jax.sharding import PartitionSpec as P

F = 4096
LAGS = 1024
BAND = 64
CAPO = 8


def whiten(raw, flags):
    values = raw.astype(jnp.float32)
    power = values[..., 0, :] ** 2 + values[..., 1, :] ** 2
    leading = power.shape[:-1]
    bands = jnp.mean(power.reshape(leading + (power.shape[-1] // BAND, BAND)), axis=-1)
    scales = jnp.repeat(lax.rsqrt(bands + 1e-06), BAND, axis=-1)
    alive = flags.astype(jnp.float32)
    return (values * scales[..., None, :] * alive[:, None, None]).astype(jnp.bfloat16)


def lag_table(count):
    freqs = jnp.arange(count, dtype=jnp.int32)
    shifts = jnp.arange(LAGS, dtype=jnp.int32) - LAGS // 2
    phase = freqs[:, None] * shifts[None, :] % (2 * F)
    theta = phase.astype(jnp.float32) * (math.pi / F)
    norm = 1.0 / math.sqrt(F)
    return (jnp.concatenate([jnp.cos(theta), -jnp.sin(theta)], axis=0) * norm).astype(jnp.bfloat16)


def cross(left, right):
    lvals = left.astype(jnp.float32)
    rvals = right.astype(jnp.float32)
    real = lvals[..., 0, :] * rvals[..., 0, :] + lvals[..., 1, :] * rvals[..., 1, :]
    imag = lvals[..., 1, :] * rvals[..., 0, :] - lvals[..., 0, :] * rvals[..., 1, :]
    return jnp.concatenate([real, imag], axis=-1).astype(jnp.bfloat16)


def shards(spectra, flags, pair_first, pair_second, owners):
    white = whiten(spectra[0], flags)
    table_full = lag_table(F)
    per_block = white.shape[0]
    blocks = lax.axis_size("stn")
    firsts = pair_first[0]
    seconds = pair_second[0]
    piece = lax.all_gather(white, "stn", axis=0, tiled=True)
    piece_rows = piece.shape[0]
    span = min(blocks, (piece_rows - 1) // per_block + 2)
    first_round = jnp.clip(jnp.int32(0) // per_block, 0, blocks - span)
    rounds = first_round + jnp.arange(span, dtype=jnp.int32)[:, None]
    local = (rounds * per_block + seconds).reshape(-1)
    inside = (local >= 0) & (local < piece_rows)
    picked = piece[jnp.clip(local, 0, piece_rows - 1)]
    keep = inside.reshape((-1,) + (1,) * (picked.ndim - 1))
    picked = jnp.where(keep, picked, jnp.zeros_like(picked))
    mine = white[firsts.reshape(-1)]
    rows = jnp.dot(cross(mine, picked), table_full, preferred_element_type=jnp.float32)
    owner = owners[0].reshape(-1)
    targets = jnp.arange(blocks, dtype=jnp.int32)
    chosen = (owner[:, None] == targets[None, :]).astype(jnp.int32)
    before = jnp.cumsum(chosen, axis=0) - chosen
    rank = jnp.sum(before * chosen, axis=1)
    outgoing = jnp.zeros((blocks, CAPO, LAGS), jnp.float32).at[owner, rank].set(rows)
    weight = 1.0 / lax.axis_size("seg")
    arrived = lax.all_to_all(
        outgoing.astype(jnp.bfloat16), "stn", split_axis=0, concat_axis=0, tiled=True
    ).astype(outgoing.dtype)
    stacked = lax.psum_scatter(
        arrived.astype(jnp.bfloat16), "seg", scatter_dimension=2, tiled=True
    ).astype(jnp.float32)
    return (stacked * weight)[None]


def solution(mesh):
    return jax.shard_map(
        shards,
        mesh=mesh,
        in_specs=(
            P("seg", "stn", None, None),
            P("stn"),
            P("stn", None, None),
            P("stn", None, None),
            P("stn", None, None, None),
        ),
        out_specs=P("stn", None, None, "seg"),
        check_vma=False,
    )
```

profile of v0, /device:TPU:1, one launch (start us, length us, event | category | flops | bytes accessed | tf_op | source)
XLA Modules:
  0.0 169.3 jit_solution(12138303990500053978)
XLA Ops:
  6.5 0.0 reduce-scatter.2.cloned.1.call-start
  6.5 0.1 add.130
  6.6 0.1 add.133
  6.7 0.1 add.131
  6.8 0.8 copy.28
  7.6 0.1 squeeze.5
  7.6 0.1 squeeze.4
  7.7 0.8 copy.25
  8.5 0.1 eq.17
  8.6 0.1 reshape_squeeze.6
  8.7 0.8 bitcast_convert_fusion
  9.5 0.1 fusion.16
  9.6 0.1 add.125
  9.7 0.1 reduce_sum.22
  9.8 0.1 broadcast_in_dim.17
  9.9 0.1 mul.87
  10.0 0.7 convert_element_type.41
  10.7 0.8 multiply_convert_fusion
  11.6 24.5 %all_gather.3 = bf16[32,2,4096]{2,1,0:T(2,128)(2,1)S(1)} all-gather(bf16[2,2,4096]{2,1,0:T(2,128)(2,1)S(1)} %multiply_convert_fusion), channel_id=1, replica_groups=mesh['stn'=16,'seg'=2] {'stn'}, dimensions={0}, use_global_device_ids=true | all-gather | bytes 557056 | tf_op jit(solution)/shard_map/all_gather | solution.py:48
  36.0 0.8 copy.27
  36.8 0.1 reshape_squeeze.7
  36.9 3.6 %gather_fusion = bf16[64,2,4096]{2,1,0:T(2,128)(2,1)} fusion(bf16[2,2,4096]{2,1,0:T(2,128)(2,1)S(1)} %multiply_convert_fusion, s32[1024]{0:T(1024)S(1)} %pad_clamp_fusion.1), kind=kCustom, calls=%fused_computation | custom fusion | bytes 2097408 | tf_op jit(solution)/shard_map/gather | solution.py:58
  40.5 2.1 %convert_element_type.43 = f32[64,2,4096]{2,1,0:T(2,128)S(1)} convert(bf16[64,2,4096]{2,1,0:T(2,128)(2,1)} %gather_fusion) | non-fusion elementwise | flops 524288 | bytes 3145728 | tf_op jit(solution)/shard_map/convert_element_type | solution.py:34
  42.6 68.4 %fusion.9 = (f32[4096,1024]{1,0:T(8,128)}, f32[4096,1024]{1,0:T(8,128)}) fusion(s32[1024]{0:T(1024)S(1)} %iota_add_fusion), kind=kLoop, calls=%fused_computation.16 | loop fusion | flops 62914560 | bytes 33558528 | tf_op jit(solution)/shard_map/cos | solution.py:30
  110.9 0.1 fusion.15
  111.0 0.1 reduce_window_sum.11
  111.1 0.2 select_reduce_fusion
  111.3 3.6 %gather_fusion.1 = bf16[64,2,4096]{2,1,0:T(2,128)(2,1)} fusion(bf16[32,2,4096]{2,1,0:T(2,128)(2,1)S(1)} %all_gather.3, s32[1024]{0:T(1024)S(1)} %pad_clamp_fusion), kind=kCustom, calls=%fused_computation.1 | custom fusion | bytes 2097408 | tf_op jit(solution)/shard_map/gather | solution.py:55
  114.9 2.2 %fusion.10 = f32[64,2,4096]{2,1,0:T(2,128)S(1)} fusion(bf16[64,2,4096]{2,1,0:T(2,128)(2,1)} %gather_fusion.1, pred[64]{0:T(512)(128)(4,1)S(1)} %compare_and_fusion), kind=kLoop, calls=%fused_computation.18 | loop fusion | flops 1048576 | bytes 3145792 | tf_op jit(solution)/shard_map/convert_element_type | solution.py:35
  117.0 3.3 %add_convert_fusion = (bf16[64,1,4096]{2,1,0:T(2,128)(2,1)S(1)}, bf16[64,1,4096]{2,1,0:T(2,128)(2,1)S(1)}) fusion(f32[64,2,4096]{2,1,0:T(2,128)S(1)} %fusion.10, f32[64,2,4096]{2,1,0:T(2,128)S(1)} %convert_element_type.43), kind=kLoop, calls=%fused_computation.23 | loop fusion | flops 2097152 | bytes 5242880 | tf_op jit(solution)/shard_map/convert.4
  120.3 1.1 copy_bitcast_fusion
  121.5 12.2 %fusion.6 = f32[64,1024]{1,0:T(8,128)S(1)} fusion(f32[4096,1024]{1,0:T(8,128)} %get-tuple-element.8, f32[4096,1024]{1,0:T(8,128)} %get-tuple-element.7, bf16[64,4096]{1,0:T(8,128)(2,1)S(1)} %get-tuple-element.9, bf16[64,4096]{1,0:T(8,128)(2,1)S(1)} %get-tuple-element.10), kind=kOutput, calls=%fused_computation.14 | convolution fusion | flops 1101004800 | bytes 34865152 | tf_op jit(solution)/shard_map/dot_general | solution.py:59
  133.8 4.0 %scatter_fusion = f32[16,8,1024]{2,1,0:T(8,128)S(1)} fusion(f32[16,8,1024]{2,1,0:T(8,128)S(1)} %broadcast_in_dim.16, s32[64]{0:T(128)S(1)} %fusion.20, f32[64,1024]{1,0:T(8,128)S(1)} %fusion.6), kind=kCustom, calls=%fused_computation.2 | custom fusion | bytes 786944 | tf_op jit(solution)/shard_map/scatter | solution.py:65
  137.8 12.8 %all_to_all.5 = bf16[16,8,1024]{2,1,0:T(8,128)(2,1)} all-to-all(bf16[16,8,1024]{2,1,0:T(8,128)(2,1)S(1)} %convert_element_type.47), channel_id=1, replica_groups=mesh['stn'=16,'seg'=2] {'stn'}, dimensions={0} | all-to-all | bytes 524288 | tf_op jit(solution)/shard_map/all_to_all | solution.py:67
  150.6 0.0 reduce-scatter.2.cloned.1.call-update
  150.7 10.1 %reduce-scatter.2.cloned.1.call-done = bf16[16,8,512]{2,1,0:T(8,128)(2,1)} async-done(((bf16[16,8,1024]{2,1,0:T(8,128)(2,1)}), bf16[16,8,512]{2,1,0:T(8,128)(2,1)}) %reduce-scatter.2.cloned.1.call-update) | async-done | bytes 131088 | tf_op jit(solution)/shard_map/reduce_scatter | solution.py:70
  160.8 1.6 multiply_bitcast_fusion
  (11 shorter events, 0.1 us)
Async XLA Ops:
  6.5 154.2 %reduce-scatter.2.cloned.1.call-start = ((), (), s32[]{:S(2)}) async-start(), calls=%async_computation.2 | async-start | bytes 393216 | tf_op jit(solution)/shard_map/reduce_scatter | solution.py:70
Sparse Core Ops, SparseCore 0:
  150.8 9.9 reduce-scatter.1
where the time goes:
time: 170 us; the launch traced here: 169 us
  other arithmetic  80.5 us (47%)
  blocking collectives  37.3 us (22%)
  local copies, waits for them, and re-layouts  15.6 us (9%)
  between operations  13.5 us (8%)
  matrix products  12.2 us (7%)
  waiting for transfers between devices  10.1 us (6%)
    cos x1, other arithmetic, lag_table(): jnp.cos(theta)  68.4 us
    all_gather x1, blocking collectives, shards(): piece = lax.all_gather(white, 'stn', axis=0, tiled=True)  24.5 us
    all_to_all x1, blocking collectives, shards(): lax.all_to_all(outgoing.astype(jnp.bfloat16), 'stn', split_axis=0, concat...  12.8 us
    dot_general x1, matrix products, shards(): jnp.dot(cross(mine, picked), table_full, preferred_element_type=jnp.float32)  12.2 us
    reduce_scatter x1, waiting for transfers between devices, shards(): lax.psum_scatter(arrived.astype(jnp.bfloat16), 'seg', scatter_dimension=2...  10.1 us
    scatter x1, local copies, waits for them, and re-layouts, shards(): jnp.zeros((blocks, CAPO, LAGS), jnp.float32).at[owner, rank].set(rows)  4.04 us
    gather x1, local copies, waits for them, and re-layouts, shards(): picked = piece[jnp.clip(local, 0, piece_rows - 1)]  3.58 us
    gather x1, local copies, waits for them, and re-layouts, shards(): mine = white[firsts.reshape(-1)]  3.58 us
  transfers between devices with their start and end apart: 1, of which 1 were waited for; matrix products, arithmetic and copies ran while one was open for 0% of the time, Pallas kernels for 0%

commit v1 on v0

v1 whole, which is shorter than its diff:
```python
import functools
import math

import jax
import jax.numpy as jnp
import numpy as np
from jax import lax
from jax.experimental import pallas as pl
from jax.experimental.pallas import tpu as pltpu
from jax.sharding import PartitionSpec as P

F = 4096
LAGS = 1024
BAND = 64
CAPO = 8
COLS = 1024
PARTS = F // COLS
ROWS = 4 * PARTS
LO = 2
CORES = 2


def lag_table(segs):
    freqs = np.arange(F, dtype=np.int64)
    shifts = np.arange(LAGS, dtype=np.int64) - LAGS // 2
    phase = freqs[:, None] * shifts[None, :] % (2 * F)
    angles = np.arange(2 * F) * (math.pi / F)
    norm = 1.0 / math.sqrt(F)
    cosines = (np.cos(angles) * norm).astype(np.float32).astype(jnp.bfloat16)
    sines = (-np.sin(angles) * norm).astype(np.float32).astype(jnp.bfloat16)
    whole = np.concatenate([cosines[phase], sines[phase]], axis=0)
    return np.ascontiguousarray(whole.reshape(2 * F, segs, LAGS // segs).transpose(1, 0, 2))


def position(core, lo, hi, his):
    return (core * LO + lo) * his + hi


def kernel(
    blocks, segs, cap,
    spectra_ref, flags_ref, meta_ref, table_ref, out_ref,
    buf, mbuf, tbl, sel, re_ref, im_ref,
    ssem, rsem, msend, mrecv, tsem,
):
    his = blocks // (LO * CORES)
    rank_out = blocks * CAPO
    depth = blocks * ROWS
    width = mbuf.shape[-1]
    stn = lax.axis_index("stn")
    seg = lax.axis_index("seg")
    core = lax.rem(stn, CORES)
    lo = lax.rem(stn // CORES, LO)
    hi = stn // (CORES * LO)
    mypos = position(core, lo, hi, his)

    def device(core, lo, hi, seg):
        return ((hi * LO + lo) * CORES + core, seg)

    z_peers = [lax.rem(hi + d, his) for d in range(1, his)]
    x_peers = [lax.rem(seg + d, segs) for d in range(1, segs)]
    z_ids = [device(core, lo, h, seg) for h in z_peers]
    x_ids = [device(core, lo, hi, s) for s in x_peers]
    y_id = device(core, 1 - lo, hi, seg)
    c_id = device(1 - core, lo, hi, seg)
    mesh_id = pl.DeviceIdType.MESH

    barrier = pltpu.get_barrier_semaphore()
    partners = z_ids + x_ids + [y_id, c_id]
    for partner in partners:
        pl.semaphore_signal(barrier, inc=1, device_id=partner, device_id_type=mesh_id)
    table_copy = pltpu.make_async_copy(table_ref.at[seg], tbl, tsem)
    table_copy.start()

    for st in range(2):
        for p in range(PARTS):
            span = pl.ds(p * COLS, COLS)
            row = pl.ds(st * PARTS + p, 1)
            re_ref[row, :] = spectra_ref[0, st, 0:1, span].astype(jnp.float32)
            im_ref[row, :] = spectra_ref[0, st, 1:2, span].astype(jnp.float32)
    re = re_ref[...]
    im = im_ref[...]
    power = re * re + im * im
    lanes = 128
    stacked = jnp.concatenate(
        [power[:, k * lanes:(k + 1) * lanes] for k in range(COLS // lanes)], axis=0
    )
    left = lax.broadcasted_iota(jnp.int32, (lanes, lanes), 0) // BAND
    right = lax.broadcasted_iota(jnp.int32, (lanes, lanes), 1) // BAND
    ones = (left == right).astype(jnp.float32)
    sums = jnp.dot(
        stacked, ones, precision=lax.Precision.HIGHEST, preferred_element_type=jnp.float32
    )
    scales = lax.rsqrt(sums * (1.0 / BAND) + 1e-06)
    per = 2 * PARTS
    scales = jnp.concatenate(
        [scales[k * per:(k + 1) * per] for k in range(COLS // lanes)], axis=1
    )
    station = lax.broadcasted_iota(jnp.int32, (per, COLS), 0) // PARTS
    alive = jnp.where(station == 0, flags_ref[0], flags_ref[1]).astype(jnp.float32)
    white = jnp.concatenate([re * scales * alive, im * scales * alive], axis=0)
    buf[seg, mypos] = white.astype(jnp.bfloat16)
    mbuf[mypos] = meta_ref[...]

    pl.semaphore_wait(barrier, len(partners))

    def data(g, pos, k, target):
        return pltpu.make_async_remote_copy(
            src_ref=buf.at[g, pos], dst_ref=buf.at[g, pos],
            send_sem=ssem.at[k], recv_sem=rsem.at[g, pos],
            device_id=target, device_id_type=mesh_id,
        )

    def forward(g, pos, k, targets):
        for target in targets:
            data(g, pos, k, target).start()
            k += 1
        return k

    def arrived(g, pos):
        data(g, pos, 0, c_id).wait_recv()

    def meta(start, count, k, recv, target):
        part = mbuf.at[pl.ds(start, count)]
        return pltpu.make_async_remote_copy(
            src_ref=part, dst_ref=part, send_sem=msend.at[k], recv_sem=mrecv.at[recv],
            device_id=target, device_id_type=mesh_id,
        )

    for d, target in enumerate(z_ids):
        meta(mypos, 1, d, d, target).start()
    k = forward(seg, mypos, 0, z_ids + x_ids + [y_id, c_id])
    froms = [lax.rem(hi + his - d, his) for d in range(1, his)]
    for d, h in enumerate(froms):
        meta(position(core, lo, h, his), 1, d, d, c_id).wait_recv()
    first = position(core, lo, 0, his)
    meta(first, his, his - 1, his - 1, y_id).start()
    for h in froms:
        pos = position(core, lo, h, his)
        arrived(seg, pos)
        k = forward(seg, pos, k, x_ids + [y_id, c_id])
    base = k
    meta(position(core, 1 - lo, 0, his), his, 0, his - 1, c_id).wait_recv()
    half = position(core, 0, 0, his)
    meta(half, LO * his, his, his, c_id).start()

    second_count = {0: 2 * his * (segs - 1), 1: his * segs}

    @pl.when(core == 0)
    def _():
        k = base
        for s in x_peers:
            for h in range(his):
                pos = position(0, lo, h, his)
                arrived(s, pos)
                k = forward(s, pos, k, [y_id, c_id])
        assert k - base == second_count[0]

    @pl.when(core == 1)
    def _():
        k = base
        for h in range(his):
            pos = position(1, 1 - lo, h, his)
            arrived(seg, pos)
            k = forward(seg, pos, k, x_ids + [c_id])
        assert k - base == second_count[1]

    meta(position(1 - core, 0, 0, his), LO * his, 0, his, c_id).wait_recv()
    firsts = mbuf[:, 0, :]
    seconds = mbuf[:, 1, :]
    owner = mbuf[:, 2, :]
    pair = lax.broadcasted_iota(jnp.int32, (blocks, width), 1)
    block = pair // cap
    block_pos = position(
        block % CORES, (block // CORES) % LO, block // (CORES * LO), his
    )
    source_pos = lax.broadcasted_iota(jnp.int32, (blocks, width), 0)
    offset = 4096
    left_row = (source_pos * ROWS + firsts * PARTS + offset).astype(jnp.float32)
    right_row = (block_pos * ROWS + seconds * PARTS + offset).astype(jnp.float32)
    mine = (owner == stn).astype(jnp.float32)
    before = (
        lax.broadcasted_iota(jnp.int32, (width, width), 0)
        < lax.broadcasted_iota(jnp.int32, (width, width), 1)
    ).astype(jnp.float32)
    rank = jnp.dot(mine, before, preferred_element_type=jnp.float32)
    slot = lax.broadcasted_iota(jnp.int32, (blocks, CAPO, width), 1).astype(jnp.float32)
    taken = jnp.where(rank[:, None, :] == slot, mine[:, None, :], 0.0)
    left_at = jnp.sum(taken * left_row[:, None, :], axis=2, keepdims=True)
    right_at = jnp.sum(taken * right_row[:, None, :], axis=2, keepdims=True)
    picks = jnp.concatenate(
        [left_at.reshape(rank_out, 1), right_at.reshape(rank_out, 1)], axis=0
    ).astype(jnp.int32) - offset
    column = lax.broadcasted_iota(jnp.int32, (2 * rank_out, depth), 1)
    gap = column - picks
    for c in range(2):
        for p in range(PARTS):
            hit = gap == c * 2 * PARTS + p
            sel[c * PARTS + p] = jnp.where(hit, 1.0, 0.0).astype(jnp.bfloat16)

    third_base = base + max(second_count.values())

    @pl.when(core == 0)
    def _():
        k = third_base
        for s in [seg] + x_peers:
            for h in range(his):
                pos = position(0, 1 - lo, h, his)
                arrived(s, pos)
                k = forward(s, pos, k, [c_id])

    @pl.when(core == 1)
    def _():
        k = third_base
        for s in x_peers:
            for l in (lo, 1 - lo):
                for h in range(his):
                    pos = position(1, l, h, his)
                    arrived(s, pos)
                    k = forward(s, pos, k, [c_id])

    for s in [seg] + x_peers:
        for l in range(LO):
            for h in range(his):
                arrived(s, position(1 - core, l, h, his))

    table_copy.wait()
    total = jnp.zeros((rank_out, out_ref.shape[-1]), jnp.float32)
    for p in range(PARTS):
        real = imag = None
        for g in range(segs):
            white = buf[g].reshape(depth, COLS)
            a = jnp.dot(sel[p], white, preferred_element_type=jnp.float32)
            b = jnp.dot(sel[PARTS + p], white, preferred_element_type=jnp.float32)
            ar, br = a[:rank_out], a[rank_out:]
            ai, bi = b[:rank_out], b[rank_out:]
            r = ar * br + ai * bi
            i = ai * br - ar * bi
            real = r if g == 0 else real + r
            imag = i if g == 0 else imag + i
        total += jnp.dot(
            real.astype(jnp.bfloat16), tbl[pl.ds(p * COLS, COLS)],
            preferred_element_type=jnp.float32,
        )
        total += jnp.dot(
            imag.astype(jnp.bfloat16), tbl[pl.ds(F + p * COLS, COLS)],
            preferred_element_type=jnp.float32,
        )
    total = total * (1.0 / segs)
    for b in range(blocks):
        pos = position(b % CORES, (b // CORES) % LO, b // (CORES * LO), his)
        out_ref[0, b] = total[pos * CAPO:(pos + 1) * CAPO]

    for d in range(his - 1):
        meta(0, 1, d, d, c_id).wait_send()
    meta(0, his, his - 1, 0, c_id).wait_send()
    meta(0, LO * his, his, 0, c_id).wait_send()

    def sent(start, count):
        for k in range(start, start + count):
            data(0, 0, k, c_id).wait_send()

    sent(0, base)

    @pl.when(core == 0)
    def _():
        sent(base, second_count[0])
        sent(third_base, his * segs)

    @pl.when(core == 1)
    def _():
        sent(base, second_count[1])
        sent(third_base, LO * his * (segs - 1))


def shards(blocks, segs, table, spectra, flags, pair_first, pair_second, owners):
    his = blocks // (LO * CORES)
    cap = pair_first.shape[-1]
    pairs = blocks * cap
    width = -(-pairs // 128) * 128
    lists = jnp.stack(
        [pair_first.reshape(pairs), pair_second.reshape(pairs), owners.reshape(pairs)]
    )
    lists = jnp.pad(lists, ((0, 5), (0, width - pairs)), constant_values=-1)
    lags = LAGS // segs
    slots = blocks * CAPO
    copies = (his - 1) + segs + 1 + (his - 1) * (segs + 1)
    copies += max(2 * his * (segs - 1), his * segs)
    copies += max(his * segs, LO * his * (segs - 1))
    vmem = pl.BlockSpec(memory_space=pltpu.VMEM)
    return pl.pallas_call(
        functools.partial(kernel, blocks, segs, cap),
        out_shape=jax.ShapeDtypeStruct((1, blocks, CAPO, lags), jnp.float32),
        in_specs=[
            vmem,
            pl.BlockSpec(memory_space=pltpu.SMEM),
            vmem,
            pl.BlockSpec(memory_space=pl.ANY),
        ],
        out_specs=vmem,
        scratch_shapes=[
            pltpu.VMEM((segs, blocks, ROWS, COLS), jnp.bfloat16),
            pltpu.VMEM((blocks, 8, width), jnp.int32),
            pltpu.VMEM((2 * F, lags), jnp.bfloat16),
            pltpu.VMEM((2 * PARTS, 2 * slots, blocks * ROWS), jnp.bfloat16),
            pltpu.VMEM((2 * PARTS, COLS), jnp.float32),
            pltpu.VMEM((2 * PARTS, COLS), jnp.float32),
            pltpu.SemaphoreType.DMA((copies,)),
            pltpu.SemaphoreType.DMA((segs, blocks)),
            pltpu.SemaphoreType.DMA((his + 1,)),
            pltpu.SemaphoreType.DMA((his + 1,)),
            pltpu.SemaphoreType.DMA,
        ],
        compiler_params=pltpu.CompilerParams(
            collective_id=0, has_side_effects=True, vmem_limit_bytes=48 * 1024 * 1024
        ),
        cost_estimate=pl.CostEstimate(
            flops=4 * slots * F * lags, bytes_accessed=4 * F * lags, transcendentals=0
        ),
    )(spectra, flags, lists, table)


def solution(mesh):
    blocks = mesh.shape["stn"]
    segs = mesh.shape["seg"]
    table = lag_table(segs)

    def program(spectra, flags, pair_first, pair_second, owners):
        return jax.shard_map(
            functools.partial(shards, blocks, segs, table),
            mesh=mesh,
            in_specs=(
                P("seg", "stn", None, None),
                P("stn"),
                P("stn", None, None),
                P("stn", None, None),
                P("stn", None, None, None),
            ),
            out_specs=P("stn", None, None, "seg"),
            check_vma=False,
        )(spectra, flags, pair_first, pair_second, owners)

    return program
```

time: 170 us -> 28.6 us (0.17)
  other arithmetic: 80.5 us -> 0.01 us
  blocking collectives: 37.3 us -> 0 us
  Pallas kernels: 0 us -> 23.6 us
  between operations: 13.5 us -> 0.04 us
  matrix products: 12.2 us -> 0 us
  local copies, waits for them, and re-layouts: 15.6 us -> 4.66 us
  waiting for transfers between devices: 10.1 us -> 0 us
    cos x1 -> x0, other arithmetic: 68.4 us -> none  [lag_table(): jnp.cos(theta)]
    all_gather x1 -> x0, blocking collectives: 24.5 us -> none  [shards(): piece = lax.all_gather(white, 'stn', axis=0, tiled=True)]
    pallas_call x0 -> x1, Pallas kernels: none -> 23.6 us  [shards(): pl.pallas_call(functools.partial(kernel, blocks, segs, cap), out_shape=ja...]
    all_to_all x1 -> x0, blocking collectives: 12.8 us -> none  [shards(): lax.all_to_all(outgoing.astype(jnp.bfloat16), 'stn', split_axis=0, concat...]
    dot_general x1 -> x0, matrix products: 12.2 us -> none  [shards(): jnp.dot(cross(mine, picked), table_full, preferred_element_type=jnp.float32)]
    reduce_scatter x1 -> x0, waiting for transfers between devices: 10.1 us -> none  [shards(): lax.psum_scatter(arrived.astype(jnp.bfloat16), 'seg', scatter_dimension=2...]
    gather x2 -> x0, local copies, waits for them, and re-layouts: 7.15 us -> none  [the longest x1 3.58 us: shards(): picked = piece[jnp.clip(local, 0, piece_rows - 1)]]
    convert_element_type x7 -> x0, other arithmetic: 6.64 us -> none  [the longest x1 2.17 us: cross(): rvals = right.astype(jnp.float32)]
  transfers between devices with their start and end apart: 1 -> 0, of which waited for: 1 -> 0; matrix products, arithmetic and copies ran while one was open for 0% -> 0% of each run, Pallas kernels for 0% -> 0%
where the time goes in v1:
time: 28.6 us; the launch traced here: 28.3 us
  Pallas kernels  23.6 us (83%)
  local copies, waits for them, and re-layouts  4.66 us (16%)
    pallas_call x1, Pallas kernels, shards(): pl.pallas_call(functools.partial(kernel, blocks, segs, cap), out_shape=ja...  23.6 us
    unnamed x8, local copies, waits for them, and re-layouts  4.39 us

profile of v1, /device:TPU:1, one launch (start us, length us, event | category | flops | bytes accessed | tf_op | source)
XLA Modules:
  0.0 28.3 jit_solution(8765867566728191152)
XLA Ops:
  0.0 0.8 %copy.10 = s32[1,16,4]{2,1,0:T(8,128)S(1)} copy(s32[1,16,4]{1,2,0:T(4,128)} %param.8) | data formatting | bytes 512 | tf_op args[2]
  0.8 0.1 stack_reshape.9
  0.8 0.8 %copy.11 = s32[1,16,4]{2,1,0:T(8,128)S(1)} copy(s32[1,16,4]{1,2,0:T(4,128)} %param.9) | data formatting | bytes 512 | tf_op args[3]
  1.6 0.1 stack_reshape.10
  1.7 0.8 %copy.12 = s32[1,16,4,1]{2,1,3,0:T(8,128)S(1)} copy(s32[1,16,4,1]{1,3,2,0:T(1,128)} %param.10) | data formatting | bytes 512 | tf_op args[4]
  2.5 0.1 stack_reshape.11
  2.6 0.0 copy-start
  2.6 0.7 %copy-done = bf16[1,2,2,4096]{3,2,1,0:T(2,128)(2,1)S(1)} copy-done((bf16[1,2,2,4096]{3,2,1,0:T(2,128)(2,1)S(1)}, bf16[1,2,2,4096]{3,2,1,0:T(2,128)(2,1)}, u32[]{:S(2)}) %copy-start) | copy-done | bytes 32792
  3.3 0.0 copy-start.1
  3.3 0.7 %copy-done.1 = s32[2]{0:T(128)S(1)} copy-done((s32[2]{0:T(128)S(1)}, s32[2]{0:T(128)}, u32[]{:S(2)}) %copy-start.1) | copy-done | bytes 32
  4.0 23.6 %shard_map.64 = f32[1,16,8,512]{3,2,1,0:T(8,128)S(1)} custom-call(bf16[1,2,2,4096]{3,2,1,0:T(2,128)(2,1)S(1)} %copy-done, s32[2]{0:T(128)S(1)} %copy-done.1, s32[8,128]{1,0:T(8,128)S(1)} %pad.4.meta_ref, bf16[2,8192,512]{2,1,0:T(8,128)(2,1)} %constant.4.clone.table_ref), custom_call_target="tpu_custom_call" | custom-call | flops 1073741824 | bytes 8388608 | tf_op jit(solution)/shard_map/pallas_call | solution.py:290
  27.6 0.7 %copy.14 = f32[1,16,8,512]{3,2,1,0:T(8,128)} copy(f32[1,16,8,512]{3,2,1,0:T(8,128)S(1)} %shard_map.64) | data formatting | bytes 524288
  (2 shorter events, 0.0 us)
Async XLA Ops:
  2.6 0.8 %copy-start = (bf16[1,2,2,4096]{3,2,1,0:T(2,128)(2,1)S(1)}, bf16[1,2,2,4096]{3,2,1,0:T(2,128)(2,1)}, u32[]{:S(2)}) copy-start(bf16[1,2,2,4096]{3,2,1,0:T(2,128)(2,1)} %spectra_ref.1) | copy-start | bytes 98308
  3.3 0.7 %copy-start.1 = (s32[2]{0:T(128)S(1)}, s32[2]{0:T(128)}, u32[]{:S(2)}) copy-start(s32[2]{0:T(128)} %flags_ref.1) | copy-start | bytes 28

commit v2 on v1

--- a/solution.py
+++ b/solution.py
@@ -38,9 +38,10 @@
 
 def kernel(
     blocks, segs, cap,
-    spectra_ref, flags_ref, meta_ref, table_ref, out_ref,
+    spectra_hbm, flags_hbm, firsts_hbm, seconds_hbm, owners_hbm, table_ref, out_ref,
+    spectra_ref, flags_ref, firsts_ref, seconds_ref, owners_ref,
     buf, mbuf, tbl, sel, re_ref, im_ref,
-    ssem, rsem, msend, mrecv, tsem,
+    ssem, rsem, msend, mrecv, tsem, isem,
 ):
     his = blocks // (LO * CORES)
     rank_out = blocks * CAPO
@@ -64,12 +65,24 @@
     c_id = device(1 - core, lo, hi, seg)
     mesh_id = pl.DeviceIdType.MESH
 
+    inputs = [
+        pltpu.make_async_copy(source, target, isem.at[n])
+        for n, (source, target) in enumerate((
+            (spectra_hbm, spectra_ref), (flags_hbm, flags_ref), (firsts_hbm, firsts_ref),
+            (seconds_hbm, seconds_ref), (owners_hbm, owners_ref),
+        ))
+    ]
+    for copy in inputs:
+        copy.start()
     barrier = pltpu.get_barrier_semaphore()
     partners = z_ids + x_ids + [y_id, c_id]
     for partner in partners:
         pl.semaphore_signal(barrier, inc=1, device_id=partner, device_id_type=mesh_id)
     table_copy = pltpu.make_async_copy(table_ref.at[seg], tbl, tsem)
     table_copy.start()
+
+    for copy in inputs:
+        copy.wait()
 
     for st in range(2):
         for p in range(PARTS):
@@ -99,7 +112,24 @@
     alive = jnp.where(station == 0, flags_ref[0], flags_ref[1]).astype(jnp.float32)
     white = jnp.concatenate([re * scales * alive, im * scales * alive], axis=0)
     buf[seg, mypos] = white.astype(jnp.bfloat16)
-    mbuf[mypos] = meta_ref[...]
+
+    spread = (
+        lax.broadcasted_iota(jnp.int32, (blocks, width), 1) % blocks
+        == lax.broadcasted_iota(jnp.int32, (blocks, width), 0)
+    ).astype(jnp.float32)
+    lane = lax.broadcasted_iota(jnp.int32, (cap, width), 1)
+    keep = lane // blocks == lax.broadcasted_iota(jnp.int32, (cap, width), 0)
+
+    def flat(listed):
+        tiled = jnp.dot(
+            listed.astype(jnp.float32), spread, preferred_element_type=jnp.float32
+        )
+        return jnp.sum(jnp.where(keep, tiled, 0.0), axis=0, keepdims=True).astype(jnp.int32)
+
+    inside = lax.broadcasted_iota(jnp.int32, (1, width), 1) < blocks * cap
+    mbuf[mypos, 0:1] = flat(firsts_ref[0])
+    mbuf[mypos, 1:2] = flat(seconds_ref[0])
+    mbuf[mypos, 2:3] = jnp.where(inside, flat(owners_ref[0, :, 0]), -1)
 
     pl.semaphore_wait(barrier, len(partners))
 
@@ -169,7 +199,7 @@
     seconds = mbuf[:, 1, :]
     owner = mbuf[:, 2, :]
     pair = lax.broadcasted_iota(jnp.int32, (blocks, width), 1)
-    block = pair // cap
+    block = pair % blocks
     block_pos = position(
         block % CORES, (block // CORES) % LO, block // (CORES * LO), his
     )
@@ -178,9 +208,10 @@
     left_row = (source_pos * ROWS + firsts * PARTS + offset).astype(jnp.float32)
     right_row = (block_pos * ROWS + seconds * PARTS + offset).astype(jnp.float32)
     mine = (owner == stn).astype(jnp.float32)
+    one = lax.broadcasted_iota(jnp.int32, (width, width), 0)
+    two = lax.broadcasted_iota(jnp.int32, (width, width), 1)
     before = (
-        lax.broadcasted_iota(jnp.int32, (width, width), 0)
-        < lax.broadcasted_iota(jnp.int32, (width, width), 1)
+        one % blocks * cap + one // blocks < two % blocks * cap + two // blocks
     ).astype(jnp.float32)
     rank = jnp.dot(mine, before, preferred_element_type=jnp.float32)
     slot = lax.broadcasted_iota(jnp.int32, (blocks, CAPO, width), 1).astype(jnp.float32)
@@ -277,10 +308,6 @@
     cap = pair_first.shape[-1]
     pairs = blocks * cap
     width = -(-pairs // 128) * 128
-    lists = jnp.stack(
-        [pair_first.reshape(pairs), pair_second.reshape(pairs), owners.reshape(pairs)]
-    )
-    lists = jnp.pad(lists, ((0, 5), (0, width - pairs)), constant_values=-1)
     lags = LAGS // segs
     slots = blocks * CAPO
     copies = (his - 1) + segs + 1 + (his - 1) * (segs + 1)
@@ -290,14 +317,14 @@
     return pl.pallas_call(
         functools.partial(kernel, blocks, segs, cap),
         out_shape=jax.ShapeDtypeStruct((1, blocks, CAPO, lags), jnp.float32),
-        in_specs=[
-            vmem,
-            pl.BlockSpec(memory_space=pltpu.SMEM),
-            vmem,
-            pl.BlockSpec(memory_space=pl.ANY),
-        ],
+        in_specs=[pl.BlockSpec(memory_space=pltpu.HBM)] * 6,
         out_specs=vmem,
         scratch_shapes=[
+            pltpu.VMEM(spectra.shape, jnp.bfloat16),
+            pltpu.SMEM(flags.shape, jnp.int32),
+            pltpu.VMEM((1, cap, blocks), jnp.int32),
+            pltpu.VMEM((1, cap, blocks), jnp.int32),
+            pltpu.VMEM((1, cap, 1, blocks), jnp.int32),
             pltpu.VMEM((segs, blocks, ROWS, COLS), jnp.bfloat16),
             pltpu.VMEM((blocks, 8, width), jnp.int32),
             pltpu.VMEM((2 * F, lags), jnp.bfloat16),
@@ -309,6 +336,7 @@
             pltpu.SemaphoreType.DMA((his + 1,)),
             pltpu.SemaphoreType.DMA((his + 1,)),
             pltpu.SemaphoreType.DMA,
+            pltpu.SemaphoreType.DMA((5,)),
         ],
         compiler_params=pltpu.CompilerParams(
             collective_id=0, has_side_effects=True, vmem_limit_bytes=48 * 1024 * 1024
@@ -316,7 +344,10 @@
         cost_estimate=pl.CostEstimate(
             flops=4 * slots * F * lags, bytes_accessed=4 * F * lags, transcendentals=0
         ),
-    )(spectra, flags, lists, table)
+    )(
+        spectra, flags, pair_first.transpose(0, 2, 1), pair_second.transpose(0, 2, 1),
+        owners.transpose(0, 2, 3, 1), table,
+    )
 
 
 def solution(mesh):

time: 28.6 us -> 27.5 us (0.962)
  Pallas kernels: 23.6 us -> 23.1 us
  local copies, waits for them, and re-layouts: 4.66 us -> 4.16 us
    pallas_call x1, Pallas kernels: 23.6 us -> 23.1 us  [shards(): pl.pallas_call(functools.partial(kernel, blocks, segs, cap), out_shape=ja...]
    unnamed x8 -> x11, local copies, waits for them, and re-layouts: 4.39 us -> 4.16 us
where the time goes in v2:
time: 27.5 us; the launch traced here: 27.3 us
  Pallas kernels  23.1 us (84%)
  local copies, waits for them, and re-layouts  4.16 us (15%)
    pallas_call x1, Pallas kernels, shards(): pl.pallas_call(functools.partial(kernel, blocks, segs, cap), out_shape=ja...  23.1 us
    unnamed x11, local copies, waits for them, and re-layouts  4.16 us

profile of v2, /device:TPU:1, one launch (start us, length us, event | category | flops | bytes accessed | tf_op | source)
XLA Modules:
  0.0 27.3 jit_solution(10835230159342183981)
XLA Ops:
  0.0 0.0 copy-start
  0.0 0.8 %copy-done = bf16[1,2,2,4096]{3,2,1,0:T(2,128)(2,1)S(1)} copy-done((bf16[1,2,2,4096]{3,2,1,0:T(2,128)(2,1)S(1)}, bf16[1,2,2,4096]{3,2,1,0:T(2,128)(2,1)}, u32[]{:S(2)}) %copy-start) | copy-done | bytes 32792
  0.8 0.0 copy-start.1
  0.8 0.7 %copy-done.1 = s32[1,16,4]{1,2,0:T(4,128)S(1)} copy-done((s32[1,16,4]{1,2,0:T(4,128)S(1)}, s32[1,16,4]{1,2,0:T(4,128)}, u32[]{:S(2)}) %copy-start.1) | copy-done | bytes 280
  1.4 0.0 copy-start.2
  1.4 0.7 %copy-done.2 = s32[1,16,4]{1,2,0:T(4,128)S(1)} copy-done((s32[1,16,4]{1,2,0:T(4,128)S(1)}, s32[1,16,4]{1,2,0:T(4,128)}, u32[]{:S(2)}) %copy-start.2) | copy-done | bytes 280
  2.1 0.0 copy-start.3
  2.1 0.7 %copy-done.3 = s32[1,16,4,1]{1,3,2,0:T(1,128)S(1)} copy-done((s32[1,16,4,1]{1,3,2,0:T(1,128)S(1)}, s32[1,16,4,1]{1,3,2,0:T(1,128)}, u32[]{:S(2)}) %copy-start.3) | copy-done | bytes 280
  2.8 0.0 copy-start.4
  2.8 0.7 %copy-done.4 = s32[2]{0:T(128)S(1)} copy-done((s32[2]{0:T(128)S(1)}, s32[2]{0:T(128)}, u32[]{:S(2)}) %copy-start.4) | copy-done | bytes 32
  3.5 23.1 %shard_map.64 = f32[1,16,8,512]{3,2,1,0:T(8,128)S(1)} custom-call(bf16[1,2,2,4096]{3,2,1,0:T(2,128)(2,1)S(1)} %copy-done, s32[2]{0:T(128)S(1)} %copy-done.4, s32[1,4,16]{2,1,0:T(4,128)S(1)} %bitcast.3, s32[1,4,16]{2,1,0:T(4,128)S(1)} %bitcast.4, s32[1,4,1,16]{3,2,1,0:T(1,128)S(1)} %bitcast.5, bf16[2,8192,512]{2,1,0:T(8,128)(2,1)} %constant.2.clone.table_ref), custom_call_target="tpu_custom_call" | custom-call | flops 1073741824 | bytes 8388608 | tf_op jit(solution)/shard_map/pallas_call | solution.py:317
  26.6 0.7 %copy.8 = f32[1,16,8,512]{3,2,1,0:T(8,128)} copy(f32[1,16,8,512]{3,2,1,0:T(8,128)S(1)} %shard_map.64) | data formatting | bytes 524288
Async XLA Ops:
  0.0 0.8 %copy-start = (bf16[1,2,2,4096]{3,2,1,0:T(2,128)(2,1)S(1)}, bf16[1,2,2,4096]{3,2,1,0:T(2,128)(2,1)}, u32[]{:S(2)}) copy-start(bf16[1,2,2,4096]{3,2,1,0:T(2,128)(2,1)} %spectra_hbm.1) | copy-start | bytes 98308
  0.8 0.7 %copy-start.1 = (s32[1,16,4]{1,2,0:T(4,128)S(1)}, s32[1,16,4]{1,2,0:T(4,128)}, u32[]{:S(2)}) copy-start(s32[1,16,4]{1,2,0:T(4,128)} %param.8) | copy-start | bytes 772
  1.4 0.7 %copy-start.2 = (s32[1,16,4]{1,2,0:T(4,128)S(1)}, s32[1,16,4]{1,2,0:T(4,128)}, u32[]{:S(2)}) copy-start(s32[1,16,4]{1,2,0:T(4,128)} %param.9) | copy-start | bytes 772
  2.1 0.7 %copy-start.3 = (s32[1,16,4,1]{1,3,2,0:T(1,128)S(1)}, s32[1,16,4,1]{1,3,2,0:T(1,128)}, u32[]{:S(2)}) copy-start(s32[1,16,4,1]{1,3,2,0:T(1,128)} %param.10) | copy-start | bytes 772
  2.8 0.7 %copy-start.4 = (s32[2]{0:T(128)S(1)}, s32[2]{0:T(128)}, u32[]{:S(2)}) copy-start(s32[2]{0:T(128)} %flags_hbm.1) | copy-start | bytes 28
